TPU v7x, 32 devices: a whole 2x2x4 slice. The times are simulated.
32 devices in a mesh: clu: 4 (over y, x), mem: 8 (over z, core).
Axes of the slice: x: 2, y: 2, z: 4, core: 2. Of those that a mesh axis runs over, the one named last changes fastest.
Arguments:
- embeddings: bfloat16 [32768, 768], P(('clu', 'mem'))
- block_order: int32 [4, 64], P('clu'), may hold values from 0 to 7, as said below
Outputs:
- weight: float32 [32768], P(('clu', 'mem'))
Inputs may be any that keep to these rules, and one draw needn't show every extreme that they name: `block_order`: each aligned run of 8 entries is a permutation of 0 to 7.
All inputs are finite; a program needn't handle non-finite values.
Results may differ from a plain program's by a relative error of at most 0.0029.
Values may be sent and summed in bfloat16 or wider, within the bound.
A program may use at most 64 MiB of HBM per device.

v0:
```python
import jax
import jax.numpy as jnp
from jax import lax
from jax.sharding import PartitionSpec as P

BLK = 128


def squared(values):
    return jnp.sum(jnp.square(values.astype(jnp.float32)), axis=1)


def class_table(count):
    spots = jnp.arange(count, dtype=jnp.int32)
    levels = count.bit_length() - 1
    classes = jnp.zeros((count,), jnp.int32)
    for level in range(1, levels + 1):
        classes = classes + (spots >= count - (count >> level)).astype(jnp.int32)
    return classes


def shards(embeddings, block_order):
    row_count = embeddings.shape[0]
    member_count = lax.axis_size("mem")
    position = lax.axis_index("mem")
    per_device = row_count // BLK
    orders = block_order[0].reshape(member_count, per_device)
    classes = class_table(per_device)
    locals_range = jnp.arange(per_device, dtype=jnp.int32)
    matches = (orders[:, :, None] == locals_range[None, None, :]).astype(jnp.int32)
    group_ids = jnp.sum(matches * classes[None, :, None], axis=1).reshape(-1)
    own_ids = jnp.repeat(
        lax.dynamic_slice_in_dim(group_ids, position * per_device, per_device), BLK
    )
    own_norms = squared(embeddings)

    def kernel_tile(other, other_row):
        other_ids = jnp.repeat(
            lax.dynamic_slice_in_dim(group_ids, other_row // BLK, per_device), BLK
        )
        products = lax.dot_general(
            embeddings, other, (((1,), (1,)), ((), ())), preferred_element_type=jnp.float32
        )
        distance = own_norms[:, None] + squared(other)[None, :] - 2.0 * products
        return jnp.where(
            own_ids[:, None] == other_ids[None, :], jnp.exp(-0.5 * distance), jnp.float32(0.0)
        )

    pieces = lax.all_gather(embeddings, "mem", axis=0, tiled=True)
    shard_count = pieces.shape[0] // row_count

    def add_shard(shard_index, running):
        shard = lax.dynamic_slice_in_dim(pieces, shard_index * row_count, row_count, 0)
        return running + jnp.sum(kernel_tile(shard, shard_index * row_count), axis=1)

    density = lax.fori_loop(0, shard_count, add_shard, jnp.zeros((row_count,), jnp.float32))
    inverse = 1.0 / density
    total = lax.psum(jnp.sum(inverse), ("clu", "mem"))
    everything = jnp.float32(row_count * lax.axis_size("clu") * member_count)
    return inverse * (everything / total)


def solution(mesh):
    placed = (P(("clu", "mem"), None), P("clu", None))
    return jax.shard_map(
        shards, mesh=mesh, in_specs=placed, out_specs=P(("clu", "mem")), check_vma=False
    )
```

profile of v0, /device:TPU:0, one launch (start us, length us, event | category | flops | bytes accessed | tf_op | source)
XLA Modules:
  0.0 225.8 jit_solution(15476375757334581380)
XLA Ops:
  6.5 0.0 all-gather.2.cloned.1.call-start
  6.5 0.7 all-gather.2.cloned.1.call-update
  7.3 0.5 broadcast.70
  7.8 1.3 reduce.3
  9.1 0.1 eq.71
  9.2 0.1 select_reduce_fusion
  9.3 0.1 reshape.24
  9.4 0.1 dynamic_slice.23
  9.4 1.8 multiply_reduce_fusion.1
  11.2 117.2 %all-gather.2.cloned.1.call-done = bf16[8192,768]{1,0:T(8,128)(2,1)} async-done(((bf16[1024,768]{1,0:T(8,128)(2,1)}), bf16[8192,768]{1,0:T(8,128)(2,1)}) %all-gather.2.cloned.1.call-update) | async-done | bytes 12582928 | tf_op jit(solution)/shard_map/all_gather | solution.py:49
  128.5 49.9 %while.16 = (s32[]{:T(128)}, f32[1024]{0:T(1024)S(1)}, s32[64]{0:T(128)S(1)}, f32[1024]{0:T(1024)S(1)}, bf16[8192,768]{1,0:T(8,128)(2,1)}, /*index=5*/bf16[1024,...) while((s32[]{:T(128)}, f32[1024]{0:T(1024)S(1)}, ...), condition=%wide.region_5.6_spmd.clone, body=%wide.region_2.5_spmd.clone.sunk | while | flops 1620312064 | bytes 4764160 | solution.py:56
  128.5 0.1 dynamic_slice.34
  128.5 0.1 broadcast_bitcast_fusion.3
  128.6 1.8 multiply_reduce_fusion.3
  130.4 4.2 %fusion.17 = f32[1024]{0:T(1024)S(1)} fusion(bf16[1024,768]{1,0:T(8,128)(2,1)} %get-tuple-element.308, f32[1024]{0:T(1024)S(1)} %multiply_reduce_fusion.3, f32[1024]{0:T(1024)S(1)} %get-tuple-element.306, s32[1024]{0:T(1024)S(1)} %get-tuple-element.271, s32[1024]{0:T(1024)S(1)} %get-tuple-element.272, bf16[8192,768]{1,0:T(8,128)(2,1)} %get-tuple-element.307, ...), kind=kOutput, calls=%fused_computation.5.clone.1 | convolution fusion | flops 1617951744 | bytes 3166212 | tf_op jit(solution)/shard_map/while/body/eval_jaxpr/dot_general | solution.py:41
  134.7 0.1 dynamic_slice.34
  134.8 0.1 broadcast_bitcast_fusion.3
  134.9 1.8 multiply_reduce_fusion.3
  136.6 4.2 %fusion.17 = f32[1024]{0:T(1024)S(1)} fusion(bf16[1024,768]{1,0:T(8,128)(2,1)} %get-tuple-element.308, f32[1024]{0:T(1024)S(1)} %multiply_reduce_fusion.3, f32[1024]{0:T(1024)S(1)} %get-tuple-element.306, s32[1024]{0:T(1024)S(1)} %get-tuple-element.271, s32[1024]{0:T(1024)S(1)} %get-tuple-element.272, bf16[8192,768]{1,0:T(8,128)(2,1)} %get-tuple-element.307, ...), kind=kOutput, calls=%fused_computation.5.clone.1 | convolution fusion | flops 1617951744 | bytes 3166212 | tf_op jit(solution)/shard_map/while/body/eval_jaxpr/dot_general | solution.py:41
  141.0 0.1 dynamic_slice.34
  141.0 0.1 broadcast_bitcast_fusion.3
  141.1 1.8 multiply_reduce_fusion.3
  142.9 4.2 %fusion.17 = f32[1024]{0:T(1024)S(1)} fusion(bf16[1024,768]{1,0:T(8,128)(2,1)} %get-tuple-element.308, f32[1024]{0:T(1024)S(1)} %multiply_reduce_fusion.3, f32[1024]{0:T(1024)S(1)} %get-tuple-element.306, s32[1024]{0:T(1024)S(1)} %get-tuple-element.271, s32[1024]{0:T(1024)S(1)} %get-tuple-element.272, bf16[8192,768]{1,0:T(8,128)(2,1)} %get-tuple-element.307, ...), kind=kOutput, calls=%fused_computation.5.clone.1 | convolution fusion | flops 1617951744 | bytes 3166212 | tf_op jit(solution)/shard_map/while/body/eval_jaxpr/dot_general | solution.py:41
  147.2 0.1 dynamic_slice.34
  147.3 0.1 broadcast_bitcast_fusion.3
  147.4 1.8 multiply_reduce_fusion.3
  149.1 4.2 %fusion.17 = f32[1024]{0:T(1024)S(1)} fusion(bf16[1024,768]{1,0:T(8,128)(2,1)} %get-tuple-element.308, f32[1024]{0:T(1024)S(1)} %multiply_reduce_fusion.3, f32[1024]{0:T(1024)S(1)} %get-tuple-element.306, s32[1024]{0:T(1024)S(1)} %get-tuple-element.271, s32[1024]{0:T(1024)S(1)} %get-tuple-element.272, bf16[8192,768]{1,0:T(8,128)(2,1)} %get-tuple-element.307, ...), kind=kOutput, calls=%fused_computation.5.clone.1 | convolution fusion | flops 1617951744 | bytes 3166212 | tf_op jit(solution)/shard_map/while/body/eval_jaxpr/dot_general | solution.py:41
  153.5 0.1 dynamic_slice.34
  153.5 0.1 broadcast_bitcast_fusion.3
  153.6 1.8 multiply_reduce_fusion.3
  155.4 4.2 %fusion.17 = f32[1024]{0:T(1024)S(1)} fusion(bf16[1024,768]{1,0:T(8,128)(2,1)} %get-tuple-element.308, f32[1024]{0:T(1024)S(1)} %multiply_reduce_fusion.3, f32[1024]{0:T(1024)S(1)} %get-tuple-element.306, s32[1024]{0:T(1024)S(1)} %get-tuple-element.271, s32[1024]{0:T(1024)S(1)} %get-tuple-element.272, bf16[8192,768]{1,0:T(8,128)(2,1)} %get-tuple-element.307, ...), kind=kOutput, calls=%fused_computation.5.clone.1 | convolution fusion | flops 1617951744 | bytes 3166212 | tf_op jit(solution)/shard_map/while/body/eval_jaxpr/dot_general | solution.py:41
  159.7 0.1 dynamic_slice.34
  159.8 0.1 broadcast_bitcast_fusion.3
  159.8 1.8 multiply_reduce_fusion.3
  161.6 4.2 %fusion.17 = f32[1024]{0:T(1024)S(1)} fusion(bf16[1024,768]{1,0:T(8,128)(2,1)} %get-tuple-element.308, f32[1024]{0:T(1024)S(1)} %multiply_reduce_fusion.3, f32[1024]{0:T(1024)S(1)} %get-tuple-element.306, s32[1024]{0:T(1024)S(1)} %get-tuple-element.271, s32[1024]{0:T(1024)S(1)} %get-tuple-element.272, bf16[8192,768]{1,0:T(8,128)(2,1)} %get-tuple-element.307, ...), kind=kOutput, calls=%fused_computation.5.clone.1 | convolution fusion | flops 1617951744 | bytes 3166212 | tf_op jit(solution)/shard_map/while/body/eval_jaxpr/dot_general | solution.py:41
  165.9 0.1 dynamic_slice.34
  166.0 0.1 broadcast_bitcast_fusion.3
  166.1 1.8 multiply_reduce_fusion.3
  167.9 4.2 %fusion.17 = f32[1024]{0:T(1024)S(1)} fusion(bf16[1024,768]{1,0:T(8,128)(2,1)} %get-tuple-element.308, f32[1024]{0:T(1024)S(1)} %multiply_reduce_fusion.3, f32[1024]{0:T(1024)S(1)} %get-tuple-element.306, s32[1024]{0:T(1024)S(1)} %get-tuple-element.271, s32[1024]{0:T(1024)S(1)} %get-tuple-element.272, bf16[8192,768]{1,0:T(8,128)(2,1)} %get-tuple-element.307, ...), kind=kOutput, calls=%fused_computation.5.clone.1 | convolution fusion | flops 1617951744 | bytes 3166212 | tf_op jit(solution)/shard_map/while/body/eval_jaxpr/dot_general | solution.py:41
  172.2 0.1 dynamic_slice.34
  172.3 0.1 broadcast_bitcast_fusion.3
  172.3 1.8 multiply_reduce_fusion.3
  174.1 4.2 %fusion.17 = f32[1024]{0:T(1024)S(1)} fusion(bf16[1024,768]{1,0:T(8,128)(2,1)} %get-tuple-element.308, f32[1024]{0:T(1024)S(1)} %multiply_reduce_fusion.3, f32[1024]{0:T(1024)S(1)} %get-tuple-element.306, s32[1024]{0:T(1024)S(1)} %get-tuple-element.271, s32[1024]{0:T(1024)S(1)} %get-tuple-element.272, bf16[8192,768]{1,0:T(8,128)(2,1)} %get-tuple-element.307, ...), kind=kOutput, calls=%fused_computation.5.clone.1 | convolution fusion | flops 1617951744 | bytes 3166212 | tf_op jit(solution)/shard_map/while/body/eval_jaxpr/dot_general | solution.py:41
  178.4 0.6 fusion.8
  179.0 38.7 %psum.7 = f32[]{:T(128)} all-reduce(f32[]{:T(128)} %fusion.8), channel_id=1, replica_groups=mesh['clu'=4,'mem'=8] {'clu','mem'}, use_global_device_ids=true, to_apply=%region_7.8 | all-reduce | flops 1 | bytes 8 | tf_op jit(solution)/shard_map/psum | solution.py:58
  218.4 0.6 broadcast_multiply_fusion
  (10 shorter events, 0.1 us)
Async XLA Ops:
  6.5 121.9 %all-gather.2.cloned.1.call-start = ((), (), s32[]{:S(2)}) async-start(), calls=%async_computation | async-start | bytes 14155776 | tf_op jit(solution)/shard_map/all_gather | solution.py:49
Sparse Core Ops, SparseCore 0:
  9.0 119.4 all-gather.1
where the time goes:
time: 227 us; the launch traced here: 226 us
  waiting for transfers between devices  118 us (52%)
  blocking collectives  38.7 us (17%)
  matrix products  33.9 us (15%)
  other arithmetic  18.7 us (8%)
  between operations  14.1 us (6%)
    all_gather x1, waiting for transfers between devices, shards(): pieces = lax.all_gather(embeddings, 'mem', axis=0, tiled=True)  117 us
    psum x1, blocking collectives, shards(): total = lax.psum(jnp.sum(inverse), ('clu', 'mem'))  38.7 us
    dot_general x8, matrix products, kernel_tile(): lax.dot_general(embeddings, other, (((1,), (1,)), ((), ())), preferred_el...  33.9 us
    reduce_sum x9, other arithmetic, squared(): return jnp.sum(jnp.square(values.astype(jnp.float32)), axis=1)  16.1 us
  transfers between devices with their start and end apart: 1, of which 1 were waited for; matrix products, arithmetic and copies ran while one was open for 2% of the time, Pallas kernels for 0%

commit v1 on v0

v1 whole, which is shorter than its diff:
```python
import functools

import jax
import jax.numpy as jnp
from jax import lax
from jax.experimental import pallas as pl
from jax.experimental.pallas import tpu as pltpu
from jax.sharding import PartitionSpec as P

BLK = 128
PER = 8
HALF = PER // 2
UNIT = 2 * BLK
MESH = pl.DeviceIdType.MESH


def kernel(
    groups, members, order_ref, emb_ref, out_ref,
    mine, buf, rowacc, colacc, hcol, result, sums, weights,
    send_sem, recv_sem, sum_send, sum_recv, back_send, back_recv,
):
    chips = members // 2
    mid = chips // 2
    clu = lax.axis_index("clu")
    mem = lax.axis_index("mem")
    chip, core = mem // 2, mem % 2

    def hub_mem(which):
        return 2 * (mid - which)

    def mirrored(which, one_chip):
        return which * (chips - 1) + (1 - 2 * which) * one_chip

    def base_and_slot(which, seen, c):
        first = which * (c // 2) * c
        per_chip = HALF * (1 - which) + which * (2 - c // 2)
        cc = c - first
        near = per_chip + cc * mid + jnp.where(seen < mid, 0, seen - mid)
        far = per_chip + per_chip * mid + cc * (mid - 1) + seen
        place = jnp.where(seen == mid, cc, jnp.where(seen < mid - 1, far, near))
        return first * chips, first * chips + place

    is_hub0 = mem == hub_mem(0)
    is_hub1 = mem == hub_mem(1)
    is_hub = jnp.logical_or(is_hub0, is_hub1)
    role = jnp.where(is_hub1, 1, 0)
    hubs = 2 * groups

    barrier = pltpu.get_barrier_semaphore()

    @pl.when(is_hub)
    def _():
        def greet(k, _):
            pl.semaphore_signal(
                barrier, inc=1, device_id=(clu, (mem + k) % members), device_id_type=MESH
            )
            return 0

        lax.fori_loop(1, members, greet, 0)

        def greet_hub(k, _):
            other = (clu + k) % groups
            for which in (0, 1):
                pl.semaphore_signal(
                    barrier, inc=1, device_id=(other, hub_mem(which)), device_id_type=MESH
                )
            return 0

        lax.fori_loop(1, groups, greet_hub, 0)

    @pl.when(jnp.logical_not(is_hub))
    def _():
        for which in (0, 1):
            pl.semaphore_signal(
                barrier, inc=1, device_id=(clu, hub_mem(which)), device_id_type=MESH
            )

    for s in range(PER):
        mine[s] = emb_ref[order_ref[0, mem * PER + s]]

    def share(which, c):
        _, slot = base_and_slot(which, mirrored(which, chip), c)
        return pltpu.make_async_remote_copy(
            src_ref=mine.at[which * HALF + c],
            dst_ref=buf.at[slot, pl.ds(pl.multiple_of(core * BLK, BLK), BLK)],
            send_sem=send_sem.at[which, c],
            recv_sem=recv_sem.at[slot, core],
            device_id=(clu, hub_mem(which)),
            device_id_type=MESH,
        )

    @pl.when(jnp.logical_not(is_hub))
    def _():
        pl.semaphore_wait(barrier, 2)
        first = jnp.where(chip < mid, 1, 0)

        def step(k, _):
            @pl.when(k < PER)
            def _():
                turn = k // HALF
                share(first * (1 - turn) + (1 - first) * turn, k % HALF).start()

            @pl.when(k >= 2)
            def _():
                done = k - 2
                turn = done // HALF
                share(first * (1 - turn) + (1 - first) * turn, done % HALF).wait_send()

            return 0

        lax.fori_loop(0, PER + 2, step, 0)

    @pl.when(is_hub)
    def _():
        pl.semaphore_wait(barrier, members - 1 + hubs - 2)
        for c in range(HALF):
            share(1 - role, c).start()
        for c in range(HALF):
            _, slot = base_and_slot(role, mid, c)
            buf[slot, :BLK] = mine[role * HALF + c]
        result[...] = jnp.zeros_like(result)

        def event(e, _):
            i = e - HALF
            j = i - HALF * mid
            idx = i % mid
            near = jnp.where(idx == 0, mid - 1, mid + idx)
            seen = jnp.where(i < 0, mid, jnp.where(j < 0, near, j % (mid - 1)))
            c = jnp.where(i < 0, e, jnp.where(j < 0, i // mid, j // (mid - 1)))
            base, slot = base_and_slot(role, seen, c)

            def arrived(half):
                pltpu.make_async_remote_copy(
                    src_ref=mine.at[0],
                    dst_ref=buf.at[slot, pl.ds(half * BLK, BLK)],
                    send_sem=send_sem.at[0, 0],
                    recv_sem=recv_sem.at[slot, half],
                    device_id=(clu, hub_mem(0)),
                    device_id_type=MESH,
                ).wait_recv()

            @pl.when(e >= HALF)
            def _():
                arrived(0)

            arrived(1)
            new = buf[slot]
            wide = new.astype(jnp.float32)
            square = wide * wide
            part = square[:, :BLK]
            for k in range(1, square.shape[1] // BLK):
                part = part + square[:, k * BLK : (k + 1) * BLK]
            hcol[slot] = jnp.broadcast_to(
                0.5 * jnp.sum(part, axis=1, keepdims=True), (UNIT, BLK)
            )
            hrow = 0.5 * jnp.sum(part.T, axis=0, keepdims=True)
            rowacc[slot] = jnp.zeros((UNIT, BLK), jnp.float32)

            def tile(q, carry):
                left, right = carry
                prod = lax.dot_general(
                    buf[q], buf[slot], (((1,), (1,)), ((), ())),
                    preferred_element_type=jnp.float32,
                )
                h = hcol[q]
                t0 = jnp.exp(prod[:, :BLK] - h - hrow[:, :BLK])
                t1 = jnp.exp(prod[:, BLK:] - h - hrow[:, BLK:])
                rowacc[q] += t0 + t1
                left = left + jnp.sum(t0.reshape(UNIT // 8, 8, BLK), axis=0)
                right = right + jnp.sum(t1.reshape(UNIT // 8, 8, BLK), axis=0)
                return left, right

            zero = jnp.zeros((8, BLK), jnp.float32)
            left, right = lax.fori_loop(base, slot + 1, tile, (zero, zero))
            colacc[slot, 0] = left
            colacc[slot, 1] = right
            rowacc[slot] = jnp.zeros((UNIT, BLK), jnp.float32)
            return 0

        lax.fori_loop(0, HALF * chips, event, 0)

        def finish(seen, _):
            holder = mirrored(role, seen)
            for c in range(HALF):
                _, slot = base_and_slot(role, seen, c)
                across = jnp.sum(rowacc[slot].T, axis=0, keepdims=True)
                for half in (0, 1):
                    density = across[:, half * BLK : (half + 1) * BLK] + jnp.sum(
                        colacc[slot, half], axis=0, keepdims=True
                    )
                    result[2 * holder + half, c : c + 1] = 1.0 / density
            return 0

        lax.fori_loop(0, chips, finish, 0)
        own = jnp.sum(result[...], axis=0)
        here = 2 * clu + role
        sums[here] = own

        def sum_copy(k, slot):
            other = (here + k) % hubs
            return pltpu.make_async_remote_copy(
                src_ref=sums.at[here],
                dst_ref=sums.at[slot],
                send_sem=sum_send.at[k],
                recv_sem=sum_recv.at[slot],
                device_id=(other // 2, hub_mem(other % 2)),
                device_id_type=MESH,
            )

        for k in range(1, hubs):
            sum_copy(k, here).start()
        for k in range(1, hubs):
            sum_copy(k, (here + k) % hubs).wait_recv()
        total = jnp.sum(jnp.sum(sums[...], axis=0), keepdims=True)
        rows = float(groups * members * PER * BLK)
        result[...] = result[...] * (rows / total)[None]

        def back(k):
            other = (mem + k) % members
            return pltpu.make_async_remote_copy(
                src_ref=result.at[other],
                dst_ref=weights.at[role],
                send_sem=back_send.at[k],
                recv_sem=back_recv.at[role],
                device_id=(clu, other),
                device_id_type=MESH,
            )

        for k in range(1, members):
            back(k).start()
        weights[role] = result[mem]
        for c in range(HALF):
            share(1 - role, c).wait_send()
        for k in range(1, hubs):
            sum_copy(k, here).wait_send()
        for k in range(1, members):
            back(k).wait_send()

    def returned(which):
        pltpu.make_async_remote_copy(
            src_ref=result.at[0],
            dst_ref=weights.at[which],
            send_sem=back_send.at[0],
            recv_sem=back_recv.at[which],
            device_id=(clu, hub_mem(which)),
            device_id_type=MESH,
        ).wait_recv()

    for which in (0, 1):
        @pl.when(mem != hub_mem(which))
        def _(which=which):
            returned(which)

    for block in range(PER):
        spot = 0
        for s in range(PER):
            spot = jnp.where(order_ref[0, mem * PER + s] == block, s, spot)
        out_ref[block : block + 1] = weights[spot // HALF, pl.ds(spot % HALF, 1)]


def solution(mesh):
    groups, members = mesh.shape["clu"], mesh.shape["mem"]

    def shards(embeddings, block_order):
        rows, width = embeddings.shape
        units = HALF * members // 2
        out = pl.pallas_call(
            functools.partial(kernel, groups, members),
            out_shape=jax.ShapeDtypeStruct((PER, BLK), jnp.float32),
            in_specs=[
                pl.BlockSpec(memory_space=pltpu.SMEM),
                pl.BlockSpec(memory_space=pltpu.VMEM),
            ],
            out_specs=pl.BlockSpec(memory_space=pltpu.VMEM),
            scratch_shapes=[
                pltpu.VMEM((PER, BLK, width), jnp.bfloat16),
                pltpu.VMEM((units, UNIT, width), jnp.bfloat16),
                pltpu.VMEM((units, UNIT, BLK), jnp.float32),
                pltpu.VMEM((units, 2, 8, BLK), jnp.float32),
                pltpu.VMEM((units, UNIT, BLK), jnp.float32),
                pltpu.VMEM((members, 8, BLK), jnp.float32),
                pltpu.VMEM((2 * groups, 8, BLK), jnp.float32),
                pltpu.VMEM((2, 8, BLK), jnp.float32),
                pltpu.SemaphoreType.DMA((2, HALF)),
                pltpu.SemaphoreType.DMA((units, 2)),
                pltpu.SemaphoreType.DMA((2 * groups,)),
                pltpu.SemaphoreType.DMA((2 * groups,)),
                pltpu.SemaphoreType.DMA((members,)),
                pltpu.SemaphoreType.DMA((2,)),
            ],
            compiler_params=pltpu.CompilerParams(
                collective_id=0, has_side_effects=True, vmem_limit_bytes=48 * 1024 * 1024
            ),
            cost_estimate=pl.CostEstimate(
                flops=2 * rows * rows * members * width // 6,
                bytes_accessed=rows * width * 2,
                transcendentals=rows * rows,
            ),
        )(block_order, embeddings.reshape(PER, BLK, width))
        return out.reshape(rows)

    return jax.shard_map(
        shards,
        mesh=mesh,
        in_specs=(P(("clu", "mem"), None), P("clu", None)),
        out_specs=P(("clu", "mem")),
        check_vma=False,
    )
```

time: 227 us -> 83 us (0.37)
  waiting for transfers between devices: 118 us -> 0 us
  Pallas kernels: 0 us -> 80.2 us
  blocking collectives: 38.7 us -> 0 us
  matrix products: 33.9 us -> 0 us
  other arithmetic: 18.7 us -> 0 us
  between operations: 14.1 us -> 0.01 us
    all_gather x1 -> x0, waiting for transfers between devices: 117 us -> none  [shards(): pieces = lax.all_gather(embeddings, 'mem', axis=0, tiled=True)]
    pallas_call x0 -> x1, Pallas kernels: none -> 80.2 us  [shards(): pl.pallas_call(functools.partial(kernel, groups, members), out_shape=jax....]
    psum x1 -> x0, blocking collectives: 38.7 us -> none  [shards(): total = lax.psum(jnp.sum(inverse), ('clu', 'mem'))]
    dot_general x8 -> x0, matrix products: 33.9 us -> none  [kernel_tile(): lax.dot_general(embeddings, other, (((1,), (1,)), ((), ())), preferred_el...]
    reduce_sum x11 -> x0, other arithmetic: 16.8 us -> none  [the longest x9 16.1 us: squared(): return jnp.sum(jnp.square(values.astype(jnp.float32)), axis=1)]
  transfers between devices with their start and end apart: 1 -> 0, of which waited for: 1 -> 0; matrix products, arithmetic and copies ran while one was open for 2% -> 0% of each run, Pallas kernels for 0% -> 0%
where the time goes in v1:
time: 83 us; the launch traced here: 82.8 us
  Pallas kernels  80.2 us (97%)
  local copies, waits for them, and re-layouts  2.66 us (3%)
    pallas_call x1, Pallas kernels, shards(): pl.pallas_call(functools.partial(kernel, groups, members), out_shape=jax....  80.2 us
    unnamed x5, local copies, waits for them, and re-layouts  2.66 us

profile of v1, /device:TPU:0, one launch (start us, length us, event | category | flops | bytes accessed | tf_op | source)
XLA Modules:
  0.0 82.8 jit_solution(4501940425039267104)
XLA Ops:
  0.0 0.0 copy-start
  0.0 1.4 %copy-done = bf16[1024,768]{1,0:T(8,128)(2,1)S(1)} copy-done((bf16[1024,768]{1,0:T(8,128)(2,1)S(1)}, bf16[1024,768]{1,0:T(8,128)(2,1)}, u32[]{:S(2)}) %copy-start) | copy-done | bytes 1572888
  1.4 0.0 copy-start.1
  1.4 0.7 copy-done.1
  2.1 80.2 %shard_map.28 = f32[8,128]{1,0:T(8,128)S(1)} custom-call(s32[1,64]{1,0:T(1,128)S(1)} %copy-done.1, bf16[8,128,768]{2,1,0:T(8,128)(2,1)S(1)} %bitcast.3), custom_call_target="tpu_custom_call" | custom-call | flops 2147483648 | bytes 1572864 | tf_op jit(solution)/shard_map/pallas_call | solution.py:267
  82.2 0.6 copy.4
Async XLA Ops:
  0.0 1.4 %copy-start = (bf16[1024,768]{1,0:T(8,128)(2,1)S(1)}, bf16[1024,768]{1,0:T(8,128)(2,1)}, u32[]{:S(2)}) copy-start(bf16[1024,768]{1,0:T(8,128)(2,1)} %param.2) | copy-start | bytes 4718596
  1.4 0.7 copy-start.1

commit v2 on v1

--- a/solution.py
+++ b/solution.py
@@ -15,8 +15,8 @@
 
 
 def kernel(
-    groups, members, order_ref, emb_ref, out_ref,
-    mine, buf, rowacc, colacc, hcol, result, sums, weights,
+    groups, members, order_hbm, emb_hbm, out_ref,
+    order_ref, emb_ref, load_sem, mine, buf, rowacc, colacc, hcol, result, sums, weights,
     send_sem, recv_sem, sum_send, sum_recv, back_send, back_recv,
 ):
     chips = members // 2
@@ -46,6 +46,10 @@
     role = jnp.where(is_hub1, 1, 0)
     hubs = 2 * groups
 
+    load_order = pltpu.make_async_copy(order_hbm, order_ref, load_sem.at[0])
+    load_emb = pltpu.make_async_copy(emb_hbm, emb_ref, load_sem.at[1])
+    load_order.start()
+    load_emb.start()
     barrier = pltpu.get_barrier_semaphore()
 
     @pl.when(is_hub)
@@ -75,6 +79,8 @@
                 barrier, inc=1, device_id=(clu, hub_mem(which)), device_id_type=MESH
             )
 
+    load_order.wait()
+    load_emb.wait()
     for s in range(PER):
         mine[s] = emb_ref[order_ref[0, mem * PER + s]]
 
@@ -156,24 +162,39 @@
             hrow = 0.5 * jnp.sum(part.T, axis=0, keepdims=True)
             rowacc[slot] = jnp.zeros((UNIT, BLK), jnp.float32)
 
-            def tile(q, carry):
-                left, right = carry
-                prod = lax.dot_general(
-                    buf[q], buf[slot], (((1,), (1,)), ((), ())),
-                    preferred_element_type=jnp.float32,
-                )
-                h = hcol[q]
-                t0 = jnp.exp(prod[:, :BLK] - h - hrow[:, :BLK])
-                t1 = jnp.exp(prod[:, BLK:] - h - hrow[:, BLK:])
-                rowacc[q] += t0 + t1
-                left = left + jnp.sum(t0.reshape(UNIT // 8, 8, BLK), axis=0)
-                right = right + jnp.sum(t1.reshape(UNIT // 8, 8, BLK), axis=0)
-                return left, right
-
-            zero = jnp.zeros((8, BLK), jnp.float32)
-            left, right = lax.fori_loop(base, slot + 1, tile, (zero, zero))
-            colacc[slot, 0] = left
-            colacc[slot, 1] = right
+            colacc[slot] = jnp.zeros((2, 8, BLK), jnp.float32)
+
+            def tiles(q, count):
+                for k in range(count):
+                    prod = lax.dot_general(
+                        buf[q + k], buf[slot], (((1,), (1,)), ((), ())),
+                        preferred_element_type=jnp.float32,
+                    )
+                    h = hcol[q + k]
+                    t0 = jnp.exp(prod[:, :BLK] - h - hrow[:, :BLK])
+                    t1 = jnp.exp(prod[:, BLK:] - h - hrow[:, BLK:])
+                    rowacc[q + k] += t0 + t1
+                    colacc[slot, 0] += jnp.sum(t0.reshape(UNIT // 8, 8, BLK), axis=0)
+                    colacc[slot, 1] += jnp.sum(t1.reshape(UNIT // 8, 8, BLK), axis=0)
+
+            count = slot + 1 - base
+            quads = count // 4
+
+            def four(k, _):
+                tiles(base + 4 * k, 4)
+                return 0
+
+            lax.fori_loop(0, quads, four, 0)
+            rest = base + 4 * quads
+
+            @pl.when(count % 4 >= 2)
+            def _():
+                tiles(rest, 2)
+
+            @pl.when(count % 2 == 1)
+            def _():
+                tiles(slot, 1)
+
             rowacc[slot] = jnp.zeros((UNIT, BLK), jnp.float32)
             return 0
 
@@ -267,12 +288,12 @@
         out = pl.pallas_call(
             functools.partial(kernel, groups, members),
             out_shape=jax.ShapeDtypeStruct((PER, BLK), jnp.float32),
-            in_specs=[
-                pl.BlockSpec(memory_space=pltpu.SMEM),
-                pl.BlockSpec(memory_space=pltpu.VMEM),
-            ],
+            in_specs=[pl.BlockSpec(memory_space=pl.ANY)] * 2,
             out_specs=pl.BlockSpec(memory_space=pltpu.VMEM),
             scratch_shapes=[
+                pltpu.SMEM(block_order.shape, jnp.int32),
+                pltpu.VMEM((PER, BLK, width), jnp.bfloat16),
+                pltpu.SemaphoreType.DMA((2,)),
                 pltpu.VMEM((PER, BLK, width), jnp.bfloat16),
                 pltpu.VMEM((units, UNIT, width), jnp.bfloat16),
                 pltpu.VMEM((units, UNIT, BLK), jnp.float32),

time: 83 us -> 68.4 us (0.82)
  Pallas kernels: 80.2 us -> 65.6 us
    pallas_call x1, Pallas kernels: 80.2 us -> 65.6 us  [shards(): pl.pallas_call(functools.partial(kernel, groups, members), out_shape=jax....]
where the time goes in v2:
time: 68.4 us; the launch traced here: 68.2 us
  Pallas kernels  65.6 us (96%)
  local copies, waits for them, and re-layouts  2.66 us (4%)
    pallas_call x1, Pallas kernels, shards(): pl.pallas_call(functools.partial(kernel, groups, members), out_shape=jax....  65.6 us
    unnamed x5, local copies, waits for them, and re-layouts  2.66 us

profile of v2, /device:TPU:0, one launch (start us, length us, event | category | flops | bytes accessed | tf_op | source)
XLA Modules:
  0.0 68.2 jit_solution(15663874989813485400)
XLA Ops:
  0.0 0.0 copy-start
  0.0 1.4 %copy-done = bf16[1024,768]{1,0:T(8,128)(2,1)S(1)} copy-done((bf16[1024,768]{1,0:T(8,128)(2,1)S(1)}, bf16[1024,768]{1,0:T(8,128)(2,1)}, u32[]{:S(2)}) %copy-start) | copy-done | bytes 1572888
  1.4 0.0 copy-start.1
  1.4 0.7 copy-done.1
  2.1 65.6 %shard_map.28 = f32[8,128]{1,0:T(8,128)S(1)} custom-call(s32[1,64]{1,0:T(1,128)S(1)} %copy-done.1, bf16[8,128,768]{2,1,0:T(8,128)(2,1)S(1)} %bitcast.3), custom_call_target="tpu_custom_call" | custom-call | flops 2147483648 | bytes 1572864 | tf_op jit(solution)/shard_map/pallas_call | solution.py:288
  67.6 0.6 copy.4
Async XLA Ops:
  0.0 1.4 %copy-start = (bf16[1024,768]{1,0:T(8,128)(2,1)S(1)}, bf16[1024,768]{1,0:T(8,128)(2,1)}, u32[]{:S(2)}) copy-start(bf16[1024,768]{1,0:T(8,128)(2,1)} %param.2) | copy-start | bytes 4718596
  1.4 0.7 copy-start.1

commit v3 on v2

--- a/solution.py
+++ b/solution.py
@@ -17,7 +17,7 @@
 def kernel(
     groups, members, order_hbm, emb_hbm, out_ref,
     order_ref, emb_ref, load_sem, mine, buf, rowacc, colacc, hcol, result, sums, weights,
-    send_sem, recv_sem, sum_send, sum_recv, back_send, back_recv,
+    partial, send_sem, recv_sem, pass_send, pass_recv, part_sem, sum_send, sum_recv, back_send, back_recv,
 ):
     chips = members // 2
     mid = chips // 2
@@ -40,11 +40,13 @@
         place = jnp.where(seen == mid, cc, jnp.where(seen < mid - 1, far, near))
         return first * chips, first * chips + place
 
-    is_hub0 = mem == hub_mem(0)
-    is_hub1 = mem == hub_mem(1)
-    is_hub = jnp.logical_or(is_hub0, is_hub1)
-    role = jnp.where(is_hub1, 1, 0)
+    hub_chip = jnp.logical_or(chip == mid, chip == mid - 1)
+    is_hub = jnp.logical_and(hub_chip, core == 0)
+    is_near = jnp.logical_and(hub_chip, core == 1)
+    role = jnp.where(chip == mid - 1, 1, 0)
     hubs = 2 * groups
+    events = HALF * chips
+    near_events = HALF + HALF * mid
 
     load_order = pltpu.make_async_copy(order_hbm, order_ref, load_sem.at[0])
     load_emb = pltpu.make_async_copy(emb_hbm, emb_ref, load_sem.at[1])
@@ -52,7 +54,7 @@
     load_emb.start()
     barrier = pltpu.get_barrier_semaphore()
 
-    @pl.when(is_hub)
+    @pl.when(hub_chip)
     def _():
         def greet(k, _):
             pl.semaphore_signal(
@@ -62,6 +64,8 @@
 
         lax.fori_loop(1, members, greet, 0)
 
+    @pl.when(is_hub)
+    def _():
         def greet_hub(k, _):
             other = (clu + k) % groups
             for which in (0, 1):
@@ -72,12 +76,14 @@
 
         lax.fori_loop(1, groups, greet_hub, 0)
 
-    @pl.when(jnp.logical_not(is_hub))
+    @pl.when(jnp.logical_not(hub_chip))
     def _():
         for which in (0, 1):
-            pl.semaphore_signal(
-                barrier, inc=1, device_id=(clu, hub_mem(which)), device_id_type=MESH
-            )
+            for half in (0, 1):
+                pl.semaphore_signal(
+                    barrier, inc=1, device_id=(clu, hub_mem(which) + half),
+                    device_id_type=MESH,
+                )
 
     load_order.wait()
     load_emb.wait()
@@ -85,19 +91,109 @@
         mine[s] = emb_ref[order_ref[0, mem * PER + s]]
 
     def share(which, c):
-        _, slot = base_and_slot(which, mirrored(which, chip), c)
+        seen = mirrored(which, chip)
+        _, slot = base_and_slot(which, seen, c)
         return pltpu.make_async_remote_copy(
             src_ref=mine.at[which * HALF + c],
             dst_ref=buf.at[slot, pl.ds(pl.multiple_of(core * BLK, BLK), BLK)],
             send_sem=send_sem.at[which, c],
             recv_sem=recv_sem.at[slot, core],
-            device_id=(clu, hub_mem(which)),
+            device_id=(clu, hub_mem(which) + jnp.where(seen < mid - 1, 0, 1)),
             device_id_type=MESH,
         )
 
-    @pl.when(jnp.logical_not(is_hub))
-    def _():
-        pl.semaphore_wait(barrier, 2)
+    def at_event(e):
+        i = e - HALF
+        j = i - HALF * mid
+        idx = i % mid
+        near = jnp.where(idx == 0, mid - 1, mid + idx)
+        seen = jnp.where(i < 0, mid, jnp.where(j < 0, near, j % (mid - 1)))
+        c = jnp.where(i < 0, e, jnp.where(j < 0, i // mid, j // (mid - 1)))
+        return base_and_slot(role, seen, c)
+
+    def arrived(slot, half):
+        pltpu.make_async_remote_copy(
+            src_ref=mine.at[0],
+            dst_ref=buf.at[slot, pl.ds(half * BLK, BLK)],
+            send_sem=send_sem.at[0, 0],
+            recv_sem=recv_sem.at[slot, half],
+            device_id=(clu, hub_mem(0)),
+            device_id_type=MESH,
+        ).wait_recv()
+
+    def passed(slot):
+        return pltpu.make_async_remote_copy(
+            src_ref=buf.at[slot],
+            dst_ref=buf.at[slot],
+            send_sem=pass_send.at[slot],
+            recv_sem=pass_recv.at[slot],
+            device_id=(clu, 2 * chip),
+            device_id_type=MESH,
+        )
+
+    part_copy = pltpu.make_async_remote_copy(
+        src_ref=partial,
+        dst_ref=partial,
+        send_sem=part_sem.at[0],
+        recv_sem=part_sem.at[1],
+        device_id=(clu, 2 * chip),
+        device_id_type=MESH,
+    )
+
+    def norms(slot):
+        wide = buf[slot].astype(jnp.float32)
+        square = wide * wide
+        part = square[:, :BLK]
+        for k in range(1, square.shape[1] // BLK):
+            part = part + square[:, k * BLK : (k + 1) * BLK]
+        hcol[slot] = jnp.broadcast_to(
+            0.5 * jnp.sum(part, axis=1, keepdims=True), (UNIT, BLK)
+        )
+        rowacc[slot] = jnp.zeros((UNIT, BLK), jnp.float32)
+        colacc[slot] = jnp.zeros((2, 8, BLK), jnp.float32)
+        return 0.5 * jnp.sum(part.T, axis=0, keepdims=True)
+
+    def compare(base, slot, hrow):
+        def tiles(q, count):
+            for k in range(count):
+                prod = lax.dot_general(
+                    buf[q + k], buf[slot], (((1,), (1,)), ((), ())),
+                    preferred_element_type=jnp.float32,
+                )
+                h = hcol[q + k]
+                t0 = jnp.exp(prod[:, :BLK] - h - hrow[:, :BLK])
+                t1 = jnp.exp(prod[:, BLK:] - h - hrow[:, BLK:])
+                rowacc[q + k] += t0 + t1
+                colacc[slot, 0] += jnp.sum(t0.reshape(UNIT // 8, 8, BLK), axis=0)
+                colacc[slot, 1] += jnp.sum(t1.reshape(UNIT // 8, 8, BLK), axis=0)
+
+        count = slot + 1 - base
+        quads = count // 4
+
+        def four(k, _):
+            tiles(base + 4 * k, 4)
+            return 0
+
+        lax.fori_loop(0, quads, four, 0)
+
+        @pl.when(count % 4 >= 2)
+        def _():
+            tiles(base + 4 * quads, 2)
+
+        @pl.when(count % 2 == 1)
+        def _():
+            tiles(slot, 1)
+
+        rowacc[slot] = jnp.zeros((UNIT, BLK), jnp.float32)
+
+    def density(slot):
+        across = jnp.sum(rowacc[slot].T, axis=0, keepdims=True)
+        down = jnp.sum(colacc[slot], axis=1)
+        return across + jnp.concatenate([down[:1], down[1:]], axis=1)
+
+    @pl.when(jnp.logical_not(hub_chip))
+    def _():
+        pl.semaphore_wait(barrier, 4)
         first = jnp.where(chip < mid, 1, 0)
 
         def step(k, _):
@@ -116,100 +212,84 @@
 
         lax.fori_loop(0, PER + 2, step, 0)
 
-    @pl.when(is_hub)
-    def _():
-        pl.semaphore_wait(barrier, members - 1 + hubs - 2)
+    @pl.when(is_near)
+    def _():
+        pl.semaphore_wait(barrier, members - 1)
         for c in range(HALF):
             share(1 - role, c).start()
         for c in range(HALF):
             _, slot = base_and_slot(role, mid, c)
-            buf[slot, :BLK] = mine[role * HALF + c]
-        result[...] = jnp.zeros_like(result)
+            buf[slot, BLK:] = mine[role * HALF + c]
+        partial[...] = jnp.zeros_like(partial)
 
         def event(e, _):
-            i = e - HALF
-            j = i - HALF * mid
-            idx = i % mid
-            near = jnp.where(idx == 0, mid - 1, mid + idx)
-            seen = jnp.where(i < 0, mid, jnp.where(j < 0, near, j % (mid - 1)))
-            c = jnp.where(i < 0, e, jnp.where(j < 0, i // mid, j // (mid - 1)))
-            base, slot = base_and_slot(role, seen, c)
-
-            def arrived(half):
-                pltpu.make_async_remote_copy(
-                    src_ref=mine.at[0],
-                    dst_ref=buf.at[slot, pl.ds(half * BLK, BLK)],
-                    send_sem=send_sem.at[0, 0],
-                    recv_sem=recv_sem.at[slot, half],
-                    device_id=(clu, hub_mem(0)),
-                    device_id_type=MESH,
-                ).wait_recv()
+            base, slot = at_event(e)
+            arrived(slot, 0)
 
             @pl.when(e >= HALF)
             def _():
-                arrived(0)
-
-            arrived(1)
-            new = buf[slot]
-            wide = new.astype(jnp.float32)
-            square = wide * wide
-            part = square[:, :BLK]
-            for k in range(1, square.shape[1] // BLK):
-                part = part + square[:, k * BLK : (k + 1) * BLK]
-            hcol[slot] = jnp.broadcast_to(
-                0.5 * jnp.sum(part, axis=1, keepdims=True), (UNIT, BLK)
-            )
-            hrow = 0.5 * jnp.sum(part.T, axis=0, keepdims=True)
-            rowacc[slot] = jnp.zeros((UNIT, BLK), jnp.float32)
-
-            colacc[slot] = jnp.zeros((2, 8, BLK), jnp.float32)
-
-            def tiles(q, count):
-                for k in range(count):
-                    prod = lax.dot_general(
-                        buf[q + k], buf[slot], (((1,), (1,)), ((), ())),
-                        preferred_element_type=jnp.float32,
-                    )
-                    h = hcol[q + k]
-                    t0 = jnp.exp(prod[:, :BLK] - h - hrow[:, :BLK])
-                    t1 = jnp.exp(prod[:, BLK:] - h - hrow[:, BLK:])
-                    rowacc[q + k] += t0 + t1
-                    colacc[slot, 0] += jnp.sum(t0.reshape(UNIT // 8, 8, BLK), axis=0)
-                    colacc[slot, 1] += jnp.sum(t1.reshape(UNIT // 8, 8, BLK), axis=0)
-
-            count = slot + 1 - base
-            quads = count // 4
-
-            def four(k, _):
-                tiles(base + 4 * k, 4)
-                return 0
-
-            lax.fori_loop(0, quads, four, 0)
-            rest = base + 4 * quads
-
-            @pl.when(count % 4 >= 2)
-            def _():
-                tiles(rest, 2)
-
-            @pl.when(count % 2 == 1)
-            def _():
-                tiles(slot, 1)
-
-            rowacc[slot] = jnp.zeros((UNIT, BLK), jnp.float32)
-            return 0
-
-        lax.fori_loop(0, HALF * chips, event, 0)
+                arrived(slot, 1)
+
+            passed(slot).start()
+            compare(base, slot, norms(slot))
+            return 0
+
+        lax.fori_loop(0, near_events, event, 0)
+
+        def fill(e, _):
+            _, slot = at_event(e)
+            partial[pl.ds(slot, 1)] = density(slot)
+            return 0
+
+        lax.fori_loop(0, near_events, fill, 0)
+        part_copy.start()
+
+        def drain(e, _):
+            _, slot = at_event(e)
+            passed(slot).wait_send()
+            return 0
+
+        lax.fori_loop(0, near_events, drain, 0)
+        for c in range(HALF):
+            share(1 - role, c).wait_send()
+        part_copy.wait_send()
+
+    @pl.when(is_hub)
+    def _():
+        pl.semaphore_wait(barrier, members - 1 + hubs - 2)
+        for c in range(HALF):
+            share(role, c).start()
+        for c in range(HALF):
+            share(1 - role, c).start()
+        result[...] = jnp.zeros_like(result)
+
+        def take(e, _):
+            _, slot = at_event(e)
+            passed(slot).wait_recv()
+            norms(slot)
+            return 0
+
+        lax.fori_loop(0, near_events, take, 0)
+
+        def event(e, _):
+            base, slot = at_event(e)
+            arrived(slot, 0)
+            arrived(slot, 1)
+            compare(base, slot, norms(slot))
+            return 0
+
+        lax.fori_loop(near_events, events, event, 0)
+        part_copy.wait_recv()
 
         def finish(seen, _):
             holder = mirrored(role, seen)
             for c in range(HALF):
                 _, slot = base_and_slot(role, seen, c)
-                across = jnp.sum(rowacc[slot].T, axis=0, keepdims=True)
+                inverse = 1.0 / (density(slot) + partial[pl.ds(slot, 1)])
                 for half in (0, 1):
-                    density = across[:, half * BLK : (half + 1) * BLK] + jnp.sum(
-                        colacc[slot, half], axis=0, keepdims=True
-                    )
-                    result[2 * holder + half, c : c + 1] = 1.0 / density
+                    result[2 * holder + half, c : c + 1] = inverse[
+                        :, half * BLK : (half + 1) * BLK
+                    ]
             return 0
 
         lax.fori_loop(0, chips, finish, 0)
@@ -251,6 +331,7 @@
             back(k).start()
         weights[role] = result[mem]
         for c in range(HALF):
+            share(role, c).wait_send()
             share(1 - role, c).wait_send()
         for k in range(1, hubs):
             sum_copy(k, here).wait_send()
@@ -302,15 +383,19 @@
                 pltpu.VMEM((members, 8, BLK), jnp.float32),
                 pltpu.VMEM((2 * groups, 8, BLK), jnp.float32),
                 pltpu.VMEM((2, 8, BLK), jnp.float32),
+                pltpu.VMEM((units, UNIT), jnp.float32),
                 pltpu.SemaphoreType.DMA((2, HALF)),
                 pltpu.SemaphoreType.DMA((units, 2)),
+                pltpu.SemaphoreType.DMA((units,)),
+                pltpu.SemaphoreType.DMA((units,)),
+                pltpu.SemaphoreType.DMA((2,)),
                 pltpu.SemaphoreType.DMA((2 * groups,)),
                 pltpu.SemaphoreType.DMA((2 * groups,)),
                 pltpu.SemaphoreType.DMA((members,)),
                 pltpu.SemaphoreType.DMA((2,)),
             ],
             compiler_params=pltpu.CompilerParams(
-                collective_id=0, has_side_effects=True, vmem_limit_bytes=48 * 1024 * 1024
+                collective_id=0, has_side_effects=True, vmem_limit_bytes=60 * 1024 * 1024
             ),
             cost_estimate=pl.CostEstimate(
                 flops=2 * rows * rows * members * width // 6,

time: 68.4 us -> 66.6 us (0.974)
  local copies, waits for them, and re-layouts: 2.66 us -> 1.28 us
    unnamed x5 -> x1, local copies, waits for them, and re-layouts: 2.66 us -> 1.28 us
where the time goes in v3:
time: 66.6 us; the launch traced here: 66.4 us
  Pallas kernels  65.1 us (98%)
  local copies, waits for them, and re-layouts  1.28 us (2%)
    pallas_call x1, Pallas kernels, shards(): pl.pallas_call(functools.partial(kernel, groups, members), out_shape=jax....  65.1 us

profile of v3, /device:TPU:0, one launch (start us, length us, event | category | flops | bytes accessed | tf_op | source)
XLA Modules:
  0.0 66.4 jit_solution(5212700346282829505)
XLA Ops:
  0.0 65.1 %shard_map.28 = f32[8,128]{1,0:T(8,128)} custom-call(s32[1,64]{1,0:T(1,128)} %order_hbm.1, bf16[8,128,768]{2,1,0:T(8,128)(2,1)} %bitcast.3), custom_call_target="tpu_custom_call" | custom-call | flops 2147483648 | bytes 1572864 | tf_op jit(solution)/shard_map/pallas_call | solution.py:369
  65.1 1.3 %copy.4 = f32[1024]{0:T(1024)} copy(f32[1024]{0:T(1024)} %bitcast.2) | data formatting | bytes 8192

commit v4 on v3

--- a/solution.py
+++ b/solution.py
@@ -202,15 +202,15 @@
                 turn = k // HALF
                 share(first * (1 - turn) + (1 - first) * turn, k % HALF).start()
 
-            @pl.when(k >= 2)
+            @pl.when(k >= HALF)
             def _():
-                done = k - 2
+                done = k - HALF
                 turn = done // HALF
                 share(first * (1 - turn) + (1 - first) * turn, done % HALF).wait_send()
 
             return 0
 
-        lax.fori_loop(0, PER + 2, step, 0)
+        lax.fori_loop(0, PER + HALF, step, 0)
 
     @pl.when(is_near)
     def _():

time: 66.6 us -> 66.6 us (level)
  no operation moved by 1% of the time
where the time goes in v4:
time: 66.6 us; the launch traced here: 66.4 us
  Pallas kernels  65.1 us (98%)
  local copies, waits for them, and re-layouts  1.28 us (2%)
    pallas_call x1, Pallas kernels, shards(): pl.pallas_call(functools.partial(kernel, groups, members), out_shape=jax....  65.1 us

profile of v4, /device:TPU:0, one launch (start us, length us, event | category | flops | bytes accessed | tf_op | source)
XLA Modules:
  0.0 66.4 jit_solution(3233114483154436739)
XLA Ops:
  0.0 65.1 %shard_map.28 = f32[8,128]{1,0:T(8,128)} custom-call(s32[1,64]{1,0:T(1,128)} %order_hbm.1, bf16[8,128,768]{2,1,0:T(8,128)(2,1)} %bitcast.3), custom_call_target="tpu_custom_call" | custom-call | flops 2147483648 | bytes 1572864 | tf_op jit(solution)/shard_map/pallas_call | solution.py:369
  65.1 1.3 %copy.4 = f32[1024]{0:T(1024)} copy(f32[1024]{0:T(1024)} %bitcast.2) | data formatting | bytes 8192

commit v5 on v4

--- a/solution.py
+++ b/solution.py
@@ -16,7 +16,7 @@
 
 def kernel(
     groups, members, order_hbm, emb_hbm, out_ref,
-    order_ref, emb_ref, load_sem, mine, buf, rowacc, colacc, hcol, result, sums, weights,
+    order_ref, emb_ref, load_sem, mine, buf, rowacc, colacc, across, hrow, result, sums, weights,
     partial, send_sem, recv_sem, pass_send, pass_recv, part_sem, sum_send, sum_recv, back_send, back_recv,
 ):
     chips = members // 2
@@ -45,6 +45,7 @@
     is_near = jnp.logical_and(hub_chip, core == 1)
     role = jnp.where(chip == mid - 1, 1, 0)
     hubs = 2 * groups
+    everyone = groups * members
     events = HALF * chips
     near_events = HALF + HALF * mid
 
@@ -54,36 +55,50 @@
     load_emb.start()
     barrier = pltpu.get_barrier_semaphore()
 
-    @pl.when(hub_chip)
-    def _():
-        def greet(k, _):
+    @pl.when(is_hub)
+    def _():
+        def greet_all(k, _):
+            flat = (clu * members + mem + k) % everyone
             pl.semaphore_signal(
-                barrier, inc=1, device_id=(clu, (mem + k) % members), device_id_type=MESH
+                barrier, inc=1, device_id=(flat // members, flat % members),
+                device_id_type=MESH,
             )
             return 0
 
-        lax.fori_loop(1, members, greet, 0)
-
-    @pl.when(is_hub)
-    def _():
-        def greet_hub(k, _):
-            other = (clu + k) % groups
+        lax.fori_loop(1, everyone, greet_all, 0)
+
+    @pl.when(jnp.logical_not(is_hub))
+    def _():
+        def greet_hub(g, _):
             for which in (0, 1):
                 pl.semaphore_signal(
-                    barrier, inc=1, device_id=(other, hub_mem(which)), device_id_type=MESH
+                    barrier, inc=1, device_id=(g, hub_mem(which)), device_id_type=MESH
                 )
             return 0
 
-        lax.fori_loop(1, groups, greet_hub, 0)
+        lax.fori_loop(0, groups, greet_hub, 0)
+
+    @pl.when(is_near)
+    def _():
+        def greet(k, _):
+            other = (mem + k) % members
+
+            @pl.when(jnp.logical_and(other != hub_mem(0), other != hub_mem(1)))
+            def _():
+                pl.semaphore_signal(
+                    barrier, inc=1, device_id=(clu, other), device_id_type=MESH
+                )
+
+            return 0
+
+        lax.fori_loop(1, members, greet, 0)
 
     @pl.when(jnp.logical_not(hub_chip))
     def _():
         for which in (0, 1):
-            for half in (0, 1):
-                pl.semaphore_signal(
-                    barrier, inc=1, device_id=(clu, hub_mem(which) + half),
-                    device_id_type=MESH,
-                )
+            pl.semaphore_signal(
+                barrier, inc=1, device_id=(clu, hub_mem(which) + 1), device_id_type=MESH
+            )
 
     load_order.wait()
     load_emb.wait()
@@ -146,26 +161,26 @@
         part = square[:, :BLK]
         for k in range(1, square.shape[1] // BLK):
             part = part + square[:, k * BLK : (k + 1) * BLK]
-        hcol[slot] = jnp.broadcast_to(
-            0.5 * jnp.sum(part, axis=1, keepdims=True), (UNIT, BLK)
-        )
-        rowacc[slot] = jnp.zeros((UNIT, BLK), jnp.float32)
+        hrow[slot] = 0.5 * jnp.sum(part.T, axis=0, keepdims=True)
         colacc[slot] = jnp.zeros((2, 8, BLK), jnp.float32)
-        return 0.5 * jnp.sum(part.T, axis=0, keepdims=True)
-
-    def compare(base, slot, hrow):
+        return 0.5 * jnp.sum(part, axis=1, keepdims=True)
+
+    def compare(base, slot, hcol):
+        rowacc[...] = jnp.zeros_like(rowacc)
+        left = jnp.broadcast_to(hcol, (UNIT, BLK))
+
         def tiles(q, count):
             for k in range(count):
                 prod = lax.dot_general(
-                    buf[q + k], buf[slot], (((1,), (1,)), ((), ())),
+                    buf[slot], buf[q + k], (((1,), (1,)), ((), ())),
                     preferred_element_type=jnp.float32,
                 )
-                h = hcol[q + k]
-                t0 = jnp.exp(prod[:, :BLK] - h - hrow[:, :BLK])
-                t1 = jnp.exp(prod[:, BLK:] - h - hrow[:, BLK:])
-                rowacc[q + k] += t0 + t1
-                colacc[slot, 0] += jnp.sum(t0.reshape(UNIT // 8, 8, BLK), axis=0)
-                colacc[slot, 1] += jnp.sum(t1.reshape(UNIT // 8, 8, BLK), axis=0)
+                h = hrow[q + k]
+                t0 = jnp.exp(prod[:, :BLK] - left - h[:, :BLK])
+                t1 = jnp.exp(prod[:, BLK:] - left - h[:, BLK:])
+                rowacc[...] += t0 + t1
+                colacc[q + k, 0] += jnp.sum(t0.reshape(UNIT // 8, 8, BLK), axis=0)
+                colacc[q + k, 1] += jnp.sum(t1.reshape(UNIT // 8, 8, BLK), axis=0)
 
         count = slot + 1 - base
         quads = count // 4
@@ -184,16 +199,16 @@
         def _():
             tiles(slot, 1)
 
-        rowacc[slot] = jnp.zeros((UNIT, BLK), jnp.float32)
+        colacc[slot] = jnp.zeros((2, 8, BLK), jnp.float32)
+        across[slot] = jnp.sum(rowacc[...].T, axis=0, keepdims=True)
 
     def density(slot):
-        across = jnp.sum(rowacc[slot].T, axis=0, keepdims=True)
         down = jnp.sum(colacc[slot], axis=1)
-        return across + jnp.concatenate([down[:1], down[1:]], axis=1)
+        return across[slot] + jnp.concatenate([down[:1], down[1:]], axis=1)
 
     @pl.when(jnp.logical_not(hub_chip))
     def _():
-        pl.semaphore_wait(barrier, 4)
+        pl.semaphore_wait(barrier, hubs + 2)
         first = jnp.where(chip < mid, 1, 0)
 
         def step(k, _):
@@ -214,7 +229,7 @@
 
     @pl.when(is_near)
     def _():
-        pl.semaphore_wait(barrier, members - 1)
+        pl.semaphore_wait(barrier, hubs + members - 3)
         for c in range(HALF):
             share(1 - role, c).start()
         for c in range(HALF):
@@ -256,7 +271,7 @@
 
     @pl.when(is_hub)
     def _():
-        pl.semaphore_wait(barrier, members - 1 + hubs - 2)
+        pl.semaphore_wait(barrier, everyone - 1)
         for c in range(HALF):
             share(role, c).start()
         for c in range(HALF):
@@ -267,6 +282,7 @@
             _, slot = at_event(e)
             passed(slot).wait_recv()
             norms(slot)
+            across[slot] = jnp.zeros((1, UNIT), jnp.float32)
             return 0
 
         lax.fori_loop(0, near_events, take, 0)
@@ -293,28 +309,7 @@
             return 0
 
         lax.fori_loop(0, chips, finish, 0)
-        own = jnp.sum(result[...], axis=0)
-        here = 2 * clu + role
-        sums[here] = own
-
-        def sum_copy(k, slot):
-            other = (here + k) % hubs
-            return pltpu.make_async_remote_copy(
-                src_ref=sums.at[here],
-                dst_ref=sums.at[slot],
-                send_sem=sum_send.at[k],
-                recv_sem=sum_recv.at[slot],
-                device_id=(other // 2, hub_mem(other % 2)),
-                device_id_type=MESH,
-            )
-
-        for k in range(1, hubs):
-            sum_copy(k, here).start()
-        for k in range(1, hubs):
-            sum_copy(k, (here + k) % hubs).wait_recv()
-        total = jnp.sum(jnp.sum(sums[...], axis=0), keepdims=True)
-        rows = float(groups * members * PER * BLK)
-        result[...] = result[...] * (rows / total)[None]
+        sums[2 * clu + role] = jnp.sum(result[...], axis=0)
 
         def back(k):
             other = (mem + k) % members
@@ -327,14 +322,33 @@
                 device_id_type=MESH,
             )
 
+        def sum_copy(k):
+            flat = (clu * members + mem + k) % everyone
+            return pltpu.make_async_remote_copy(
+                src_ref=sums.at[2 * clu + role],
+                dst_ref=sums.at[2 * clu + role],
+                send_sem=sum_send.at[k],
+                recv_sem=sum_recv.at[2 * clu + role],
+                device_id=(flat // members, flat % members),
+                device_id_type=MESH,
+            )
+
+        def tell(k, _):
+            sum_copy(k).start()
+            return 0
+
+        def told(k, _):
+            sum_copy(k).wait_send()
+            return 0
+
+        lax.fori_loop(1, everyone, tell, 0)
         for k in range(1, members):
             back(k).start()
         weights[role] = result[mem]
         for c in range(HALF):
             share(role, c).wait_send()
             share(1 - role, c).wait_send()
-        for k in range(1, hubs):
-            sum_copy(k, here).wait_send()
+        lax.fori_loop(1, everyone, told, 0)
         for k in range(1, members):
             back(k).wait_send()
 
@@ -353,11 +367,25 @@
         def _(which=which):
             returned(which)
 
+    for one in range(hubs):
+        @pl.when(jnp.logical_or(clu != one // 2, mem != hub_mem(one % 2)))
+        def _(one=one):
+            pltpu.make_async_remote_copy(
+                src_ref=sums.at[one],
+                dst_ref=sums.at[one],
+                send_sem=sum_send.at[0],
+                recv_sem=sum_recv.at[one],
+                device_id=(clu, hub_mem(0)),
+                device_id_type=MESH,
+            ).wait_recv()
+
+    total = jnp.sum(jnp.sum(sums[...], axis=0), keepdims=True)
+    scale = float(everyone * PER * BLK) / total
     for block in range(PER):
         spot = 0
         for s in range(PER):
             spot = jnp.where(order_ref[0, mem * PER + s] == block, s, spot)
-        out_ref[block : block + 1] = weights[spot // HALF, pl.ds(spot % HALF, 1)]
+        out_ref[block : block + 1] = weights[spot // HALF, pl.ds(spot % HALF, 1)] * scale
 
 
 def solution(mesh):
@@ -377,9 +405,10 @@
                 pltpu.SemaphoreType.DMA((2,)),
                 pltpu.VMEM((PER, BLK, width), jnp.bfloat16),
                 pltpu.VMEM((units, UNIT, width), jnp.bfloat16),
-                pltpu.VMEM((units, UNIT, BLK), jnp.float32),
+                pltpu.VMEM((UNIT, BLK), jnp.float32),
                 pltpu.VMEM((units, 2, 8, BLK), jnp.float32),
-                pltpu.VMEM((units, UNIT, BLK), jnp.float32),
+                pltpu.VMEM((units, 1, UNIT), jnp.float32),
+                pltpu.VMEM((units, 1, UNIT), jnp.float32),
                 pltpu.VMEM((members, 8, BLK), jnp.float32),
                 pltpu.VMEM((2 * groups, 8, BLK), jnp.float32),
                 pltpu.VMEM((2, 8, BLK), jnp.float32),
@@ -389,7 +418,7 @@
                 pltpu.SemaphoreType.DMA((units,)),
                 pltpu.SemaphoreType.DMA((units,)),
                 pltpu.SemaphoreType.DMA((2,)),
-                pltpu.SemaphoreType.DMA((2 * groups,)),
+                pltpu.SemaphoreType.DMA((groups * members,)),
                 pltpu.SemaphoreType.DMA((2 * groups,)),
                 pltpu.SemaphoreType.DMA((members,)),
                 pltpu.SemaphoreType.DMA((2,)),

time: 66.6 us -> 52.6 us (0.79)
  Pallas kernels: 65.1 us -> 51.1 us
    pallas_call x1, Pallas kernels: 65.1 us -> 51.1 us  [shards(): pl.pallas_call(functools.partial(kernel, groups, members), out_shape=jax....]
where the time goes in v5:
time: 52.6 us; the launch traced here: 52.4 us
  Pallas kernels  51.1 us (97%)
  local copies, waits for them, and re-layouts  1.28 us (2%)
    pallas_call x1, Pallas kernels, shards(): pl.pallas_call(functools.partial(kernel, groups, members), out_shape=jax....  51.1 us
    unnamed x1, local copies, waits for them, and re-layouts  1.28 us

profile of v5, /device:TPU:0, one launch (start us, length us, event | category | flops | bytes accessed | tf_op | source)
XLA Modules:
  0.0 52.4 jit_solution(11131247649392802156)
XLA Ops:
  0.0 51.1 %shard_map.28 = f32[8,128]{1,0:T(8,128)} custom-call(s32[1,64]{1,0:T(1,128)} %order_hbm.1, bf16[8,128,768]{2,1,0:T(8,128)(2,1)} %bitcast.3), custom_call_target="tpu_custom_call" | custom-call | flops 2147483648 | bytes 1572864 | tf_op jit(solution)/shard_map/pallas_call | solution.py:397
  51.1 1.3 %copy.4 = f32[1024]{0:T(1024)} copy(f32[1024]{0:T(1024)} %bitcast.2) | data formatting | bytes 8192

commit v6 on v5

--- a/solution.py
+++ b/solution.py
@@ -16,7 +16,7 @@
 
 def kernel(
     groups, members, order_hbm, emb_hbm, out_ref,
-    order_ref, emb_ref, load_sem, mine, buf, rowacc, colacc, across, hrow, result, sums, weights,
+    order_ref, emb_ref, load_sem, mine, buf, turned, rowacc, colacc, across, hrow, result, sums, weights,
     partial, send_sem, recv_sem, pass_send, pass_recv, part_sem, sum_send, sum_recv, back_send, back_recv,
 ):
     chips = members // 2
@@ -157,6 +157,7 @@
 
     def norms(slot):
         wide = buf[slot].astype(jnp.float32)
+        turned[slot] = wide.T.astype(jnp.bfloat16)
         square = wide * wide
         part = square[:, :BLK]
         for k in range(1, square.shape[1] // BLK):
@@ -172,7 +173,7 @@
         def tiles(q, count):
             for k in range(count):
                 prod = lax.dot_general(
-                    buf[slot], buf[q + k], (((1,), (1,)), ((), ())),
+                    buf[slot], turned[q + k], (((1,), (0,)), ((), ())),
                     preferred_element_type=jnp.float32,
                 )
                 h = hrow[q + k]
@@ -405,6 +406,7 @@
                 pltpu.SemaphoreType.DMA((2,)),
                 pltpu.VMEM((PER, BLK, width), jnp.bfloat16),
                 pltpu.VMEM((units, UNIT, width), jnp.bfloat16),
+                pltpu.VMEM((units, width, UNIT), jnp.bfloat16),
                 pltpu.VMEM((UNIT, BLK), jnp.float32),
                 pltpu.VMEM((units, 2, 8, BLK), jnp.float32),
                 pltpu.VMEM((units, 1, UNIT), jnp.float32),
@@ -424,7 +426,7 @@
                 pltpu.SemaphoreType.DMA((2,)),
             ],
             compiler_params=pltpu.CompilerParams(
-                collective_id=0, has_side_effects=True, vmem_limit_bytes=60 * 1024 * 1024
+                collective_id=0, has_side_effects=True, vmem_limit_bytes=58 * 1024 * 1024
             ),
             cost_estimate=pl.CostEstimate(
                 flops=2 * rows * rows * members * width // 6,

time: 52.6 us -> 52.5 us (level)
  no operation moved by 1% of the time
where the time goes in v6:
time: 52.5 us; the launch traced here: 52.3 us
  Pallas kernels  51 us (97%)
  local copies, waits for them, and re-layouts  1.28 us (2%)
    pallas_call x1, Pallas kernels, shards(): pl.pallas_call(functools.partial(kernel, groups, members), out_shape=jax....  51 us
    unnamed x1, local copies, waits for them, and re-layouts  1.28 us

profile of v6, /device:TPU:0, one launch (start us, length us, event | category | flops | bytes accessed | tf_op | source)
XLA Modules:
  0.0 52.3 jit_solution(1442676830183417503)
XLA Ops:
  0.0 51.0 %shard_map.28 = f32[8,128]{1,0:T(8,128)} custom-call(s32[1,64]{1,0:T(1,128)} %order_hbm.1, bf16[8,128,768]{2,1,0:T(8,128)(2,1)} %bitcast.3), custom_call_target="tpu_custom_call" | custom-call | flops 2147483648 | bytes 1572864 | tf_op jit(solution)/shard_map/pallas_call | solution.py:398
  51.0 1.3 %copy.4 = f32[1024]{0:T(1024)} copy(f32[1024]{0:T(1024)} %bitcast.2) | data formatting | bytes 8192

commit v7 on v6

--- a/solution.py
+++ b/solution.py
@@ -102,8 +102,9 @@
 
     load_order.wait()
     load_emb.wait()
-    for s in range(PER):
-        mine[s] = emb_ref[order_ref[0, mem * PER + s]]
+
+    def fetch(s):
+        return emb_ref[order_ref[0, mem * PER + s]]
 
     def share(which, c):
         seen = mirrored(which, chip)
@@ -216,7 +217,9 @@
             @pl.when(k < PER)
             def _():
                 turn = k // HALF
-                share(first * (1 - turn) + (1 - first) * turn, k % HALF).start()
+                which = first * (1 - turn) + (1 - first) * turn
+                mine[which * HALF + k % HALF] = fetch(which * HALF + k % HALF)
+                share(which, k % HALF).start()
 
             @pl.when(k >= HALF)
             def _():
@@ -232,10 +235,11 @@
     def _():
         pl.semaphore_wait(barrier, hubs + members - 3)
         for c in range(HALF):
+            mine[(1 - role) * HALF + c] = fetch((1 - role) * HALF + c)
             share(1 - role, c).start()
         for c in range(HALF):
             _, slot = base_and_slot(role, mid, c)
-            buf[slot, BLK:] = mine[role * HALF + c]
+            buf[slot, BLK:] = fetch(role * HALF + c)
         partial[...] = jnp.zeros_like(partial)
 
         def event(e, _):
@@ -273,10 +277,10 @@
     @pl.when(is_hub)
     def _():
         pl.semaphore_wait(barrier, everyone - 1)
-        for c in range(HALF):
-            share(role, c).start()
-        for c in range(HALF):
-            share(1 - role, c).start()
+        for which in (1 - role, role):
+            for c in range(HALF):
+                mine[which * HALF + c] = fetch(which * HALF + c)
+                share(which, c).start()
         result[...] = jnp.zeros_like(result)
 
         def take(e, _):
@@ -310,7 +314,8 @@
             return 0
 
         lax.fori_loop(0, chips, finish, 0)
-        sums[2 * clu + role] = jnp.sum(result[...], axis=0)
+        own = jnp.sum(jnp.sum(result[...], axis=0), axis=0, keepdims=True)
+        result[:, HALF : HALF + 1] = jnp.broadcast_to(own[None], (members, 1, BLK))
 
         def back(k):
             other = (mem + k) % members
@@ -324,9 +329,9 @@
             )
 
         def sum_copy(k):
-            flat = (clu * members + mem + k) % everyone
+            flat = (clu * members + k) % everyone
             return pltpu.make_async_remote_copy(
-                src_ref=sums.at[2 * clu + role],
+                src_ref=result.at[mem],
                 dst_ref=sums.at[2 * clu + role],
                 send_sem=sum_send.at[k],
                 recv_sem=sum_recv.at[2 * clu + role],
@@ -342,14 +347,14 @@
             sum_copy(k).wait_send()
             return 0
 
-        lax.fori_loop(1, everyone, tell, 0)
+        lax.fori_loop(members, everyone, tell, 0)
         for k in range(1, members):
             back(k).start()
         weights[role] = result[mem]
         for c in range(HALF):
             share(role, c).wait_send()
             share(1 - role, c).wait_send()
-        lax.fori_loop(1, everyone, told, 0)
+        lax.fori_loop(members, everyone, told, 0)
         for k in range(1, members):
             back(k).wait_send()
 
@@ -369,7 +374,11 @@
             returned(which)
 
     for one in range(hubs):
-        @pl.when(jnp.logical_or(clu != one // 2, mem != hub_mem(one % 2)))
+        @pl.when(clu == one // 2)
+        def _(one=one):
+            sums[one] = weights[one % 2]
+
+        @pl.when(clu != one // 2)
         def _(one=one):
             pltpu.make_async_remote_copy(
                 src_ref=sums.at[one],
@@ -380,7 +389,7 @@
                 device_id_type=MESH,
             ).wait_recv()
 
-    total = jnp.sum(jnp.sum(sums[...], axis=0), keepdims=True)
+    total = jnp.sum(jnp.sum(sums[...], axis=0)[HALF : HALF + 1], keepdims=True)
     scale = float(everyone * PER * BLK) / total
     for block in range(PER):
         spot = 0

time: 52.5 us -> 52.3 us (level)
  no operation moved by 1% of the time
where the time goes in v7:
time: 52.3 us; the launch traced here: 52.1 us
  Pallas kernels  50.9 us (97%)
  local copies, waits for them, and re-layouts  1.28 us (2%)
    pallas_call x1, Pallas kernels, shards(): pl.pallas_call(functools.partial(kernel, groups, members), out_shape=jax....  50.9 us
    unnamed x1, local copies, waits for them, and re-layouts  1.28 us

profile of v7, /device:TPU:0, one launch (start us, length us, event | category | flops | bytes accessed | tf_op | source)
XLA Modules:
  0.0 52.1 jit_solution(15247978595938777689)
XLA Ops:
  0.0 50.9 %shard_map.28 = f32[8,128]{1,0:T(8,128)} custom-call(s32[1,64]{1,0:T(1,128)} %order_hbm.1, bf16[8,128,768]{2,1,0:T(8,128)(2,1)} %bitcast.3), custom_call_target="tpu_custom_call" | custom-call | flops 2147483648 | bytes 1572864 | tf_op jit(solution)/shard_map/pallas_call | solution.py:407
  50.9 1.3 %copy.4 = f32[1024]{0:T(1024)} copy(f32[1024]{0:T(1024)} %bitcast.2) | data formatting | bytes 8192

commit v8 on v7

--- a/solution.py
+++ b/solution.py
@@ -242,8 +242,7 @@
             buf[slot, BLK:] = fetch(role * HALF + c)
         partial[...] = jnp.zeros_like(partial)
 
-        def event(e, _):
-            base, slot = at_event(e)
+        def receive(slot, e):
             arrived(slot, 0)
 
             @pl.when(e >= HALF)
@@ -251,10 +250,25 @@
                 arrived(slot, 1)
 
             passed(slot).start()
+
+        def event(e, _):
+            base, slot = at_event(e)
+            receive(slot, e)
             compare(base, slot, norms(slot))
             return 0
 
-        lax.fori_loop(0, near_events, event, 0)
+        def forward(e, _):
+            receive(at_event(e)[1], e)
+            return 0
+
+        def late_event(e, _):
+            base, slot = at_event(e)
+            compare(base, slot, norms(slot))
+            return 0
+
+        lax.fori_loop(0, near_events - HALF, event, 0)
+        lax.fori_loop(near_events - HALF, near_events, forward, 0)
+        lax.fori_loop(near_events - HALF, near_events, late_event, 0)
 
         def fill(e, _):
             _, slot = at_event(e)

time: 52.3 us -> 52.3 us (level)
  no operation moved by 1% of the time
where the time goes in v8:
time: 52.3 us; the launch traced here: 52.1 us
  Pallas kernels  50.8 us (97%)
  local copies, waits for them, and re-layouts  1.28 us (2%)
    pallas_call x1, Pallas kernels, shards(): pl.pallas_call(functools.partial(kernel, groups, members), out_shape=jax....  50.8 us
    unnamed x1, local copies, waits for them, and re-layouts  1.28 us

profile of v8, /device:TPU:0, one launch (start us, length us, event | category | flops | bytes accessed | tf_op | source)
XLA Modules:
  0.0 52.1 jit_solution(10270973428762650923)
XLA Ops:
  0.0 50.8 %shard_map.28 = f32[8,128]{1,0:T(8,128)} custom-call(s32[1,64]{1,0:T(1,128)} %order_hbm.1, bf16[8,128,768]{2,1,0:T(8,128)(2,1)} %bitcast.3), custom_call_target="tpu_custom_call" | custom-call | flops 2147483648 | bytes 1572864 | tf_op jit(solution)/shard_map/pallas_call | solution.py:421
  50.9 1.3 %copy.4 = f32[1024]{0:T(1024)} copy(f32[1024]{0:T(1024)} %bitcast.2) | data formatting | bytes 8192

commit v9 on v6

--- a/solution.py
+++ b/solution.py
@@ -426,7 +426,7 @@
                 pltpu.SemaphoreType.DMA((2,)),
             ],
             compiler_params=pltpu.CompilerParams(
-                collective_id=0, has_side_effects=True, vmem_limit_bytes=58 * 1024 * 1024
+                collective_id=0, has_side_effects=True, vmem_limit_bytes=53 * 1024 * 1024
             ),
             cost_estimate=pl.CostEstimate(
                 flops=2 * rows * rows * members * width // 6,

time: 52.5 us -> 51.8 us (0.987)
  Pallas kernels: 51 us -> 50.4 us
    pallas_call x1, Pallas kernels: 51 us -> 50.4 us  [shards(): pl.pallas_call(functools.partial(kernel, groups, members), out_shape=jax....]
    unnamed x1 -> x3, local copies, waits for them, and re-layouts: 1.28 us -> 1.25 us
where the time goes in v9:
time: 51.8 us; the launch traced here: 51.7 us
  Pallas kernels  50.4 us (97%)
  local copies, waits for them, and re-layouts  1.25 us (2%)
    pallas_call x1, Pallas kernels, shards(): pl.pallas_call(functools.partial(kernel, groups, members), out_shape=jax....  50.4 us
    unnamed x3, local copies, waits for them, and re-layouts  1.25 us

profile of v9, /device:TPU:0, one launch (start us, length us, event | category | flops | bytes accessed | tf_op | source)
XLA Modules:
  0.0 51.7 jit_solution(7232634098122177452)
XLA Ops:
  0.0 0.0 copy-start
  0.0 0.7 %copy-done = s32[1,64]{1,0:T(1,128)S(1)} copy-done((s32[1,64]{1,0:T(1,128)S(1)}, s32[1,64]{1,0:T(1,128)}, u32[]{:S(2)}) %copy-start) | copy-done | bytes 280
  0.7 50.4 %shard_map.28 = f32[8,128]{1,0:T(8,128)S(1)} custom-call(s32[1,64]{1,0:T(1,128)S(1)} %copy-done, bf16[8,128,768]{2,1,0:T(8,128)(2,1)} %bitcast.3), custom_call_target="tpu_custom_call" | custom-call | flops 2147483648 | bytes 1572864 | tf_op jit(solution)/shard_map/pallas_call | solution.py:398
  51.1 0.6 %copy.4 = f32[1024]{0:T(1024)} copy(f32[1024]{0:T(1024)S(1)} %bitcast.2) | data formatting | bytes 8192
Async XLA Ops:
  0.0 0.7 %copy-start = (s32[1,64]{1,0:T(1,128)S(1)}, s32[1,64]{1,0:T(1,128)}, u32[]{:S(2)}) copy-start(s32[1,64]{1,0:T(1,128)} %order_hbm.1) | copy-start | bytes 772
